TPU v7x, 32 devices: a whole 2x2x4 slice. The times are simulated.
32 devices in a mesh: space: 8 (over y, x, core), chan: 4 (over z).
Axes of the slice: x: 2, y: 2, z: 4, core: 2. Of those that a mesh axis runs over, the one named last changes fastest.
Arguments:
- voxels: bfloat16 [32, 16, 16, 512], P(None, 'space'), may hold values from -6 to 6
- first_filters: bfloat16 [3, 3, 3, 64, 32], P(None, None, None, 'chan'), may hold values from -0.21875 to 0.21875
- second_filters: bfloat16 [3, 3, 3, 64, 64], P(None, None, None, 'chan'), may hold values from -0.15625 to 0.15625
Outputs:
- filtered: bfloat16 [64, 16, 16, 512], P('chan', 'space')
All inputs are finite; a program needn't handle non-finite values.
Results may differ from a plain program's by a relative error of at most 0.0049.
Values may be sent and summed in bfloat16 or wider, within the bound.
A program may use at most 64 MiB of HBM per device.

v0:
```python
import jax
import jax.numpy as jnp
from jax import lax
from jax.sharding import PartitionSpec as P

GH = 8


def passed_along(value, axis, steps):
    count = lax.axis_size(axis)
    pairs = [(source, (source + steps) % count) for source in range(count)]
    return lax.ppermute(value, axis, pairs)


def extended(value, sides, width):
    for axis, dim in sides:
        size, length = (lax.axis_size(axis), value.shape[dim])
        up = [(i, (i + 1) % size) for i in range(size - 1)]
        down = [(j, i) for i, j in up]
        last = lax.slice_in_dim(value, length - width, length, axis=dim)
        initial = lax.slice_in_dim(value, 0, width, axis=dim)
        before = lax.ppermute(last, axis, up)
        after = lax.ppermute(initial, axis, down)
        value = jnp.concatenate([before, value, after], axis=dim)
    return value


def stack_taps(sided):
    return jnp.concatenate([sided[..., :-2], sided[..., 1:-1], sided[..., 2:]], 0)


def tile_border(volume_tile, above, below, front, back):
    tile_count = lax.axis_size("space")
    position = (lax.axis_index("space") + GH + GH // 4) % tile_count
    tile_row = position % GH
    depth_tile = position // GH
    grid_depth = tile_count // GH
    above_rim = above(volume_tile[:, :, -1:, :])
    below_rim = below(volume_tile[:, :, :1, :])
    above_rim = jnp.where(tile_row > 0, above_rim, jnp.zeros_like(above_rim))
    below_rim = jnp.where(tile_row < GH - 1, below_rim, jnp.zeros_like(below_rim))
    taller = jnp.concatenate([above_rim, volume_tile, below_rim], 2)
    front_rim = front(taller[:, -1:])
    back_rim = back(taller[:, :1])
    front_rim = jnp.where(depth_tile > 0, front_rim, jnp.zeros_like(front_rim))
    back_rim = jnp.where(depth_tile < grid_depth - 1, back_rim, jnp.zeros_like(back_rim))
    return jnp.concatenate([front_rim, taller, back_rim], 1)


def input_above(rim_cells):
    return passed_along(rim_cells, "space", 1)


def input_below(rim_cells):
    return passed_along(rim_cells, "space", -1)


def input_front(rim_cells):
    return passed_along(rim_cells, "space", GH)


def input_back(rim_cells):
    return passed_along(rim_cells, "space", -GH)


def hidden_above(rim_cells):
    return passed_along(rim_cells, "space", 1)


def hidden_below(rim_cells):
    return passed_along(rim_cells, "space", -1)


def hidden_front(rim_cells):
    return passed_along(rim_cells, "space", GH)


def hidden_back(rim_cells):
    return passed_along(rim_cells, "space", -GH)


def correlate(stacked, filters, depth_rows, height_rows):
    out_count = filters.shape[3]
    running = jnp.zeros((out_count, depth_rows, height_rows, stacked.shape[3]), jnp.float32)
    for depth_tap in range(3):
        for height_tap in range(3):
            matrix = filters[depth_tap, height_tap].transpose(1, 0, 2).reshape(out_count, -1)
            window = stacked[
                :, depth_tap : depth_tap + depth_rows, height_tap : height_tap + height_rows, :
            ]
            running = running + jnp.einsum(
                "ok,kdhw->odhw", matrix, window, preferred_element_type=jnp.float32
            )
    return running


def local(voxels, first_filters, second_filters):
    depth_rows = voxels.shape[1]
    height_rows = voxels.shape[2]
    width_cells = voxels.shape[3]
    share = width_cells // lax.axis_size("chan")
    own_cols = lax.dynamic_slice_in_dim(voxels, lax.axis_index("chan") * share, share, 3)
    every_first, every_second = (
        lax.all_gather(first_filters, "chan", axis=3, tiled=True),
        lax.all_gather(second_filters, "chan", axis=3, tiled=True),
    )
    sided = extended(own_cols, (("chan", 3),), 1)
    padded = tile_border(sided, input_above, input_below, input_front, input_back)
    hidden = jax.nn.relu(
        correlate(stack_taps(padded), every_first, depth_rows, height_rows)
    ).astype(jnp.bfloat16)
    hidden_sided = extended(hidden, (("chan", 3),), 1)
    hidden_pad = tile_border(hidden_sided, hidden_above, hidden_below, hidden_front, hidden_back)
    result = jax.nn.relu(
        correlate(stack_taps(hidden_pad), every_second, depth_rows, height_rows)
    ).astype(jnp.bfloat16)
    return lax.all_to_all(result, "chan", split_axis=0, concat_axis=3, tiled=True)


def solution(mesh):
    return jax.shard_map(
        local,
        mesh=mesh,
        in_specs=(
            P(None, "space", None, None),
            P(None, None, None, "chan", None),
            P(None, None, None, "chan", None),
        ),
        out_specs=P("chan", "space", None, None),
        check_vma=False,
    )
```

profile of v0, /device:TPU:0, one launch (start us, length us, event | category | flops | bytes accessed | tf_op | source)
XLA Modules:
  0.0 122.0 jit_solution(9485537996072890360)
XLA Ops:
  0.0 1.2 %copy-done = bf16[32,2,16,512]{3,2,1,0:T(8,128)(2,1)S(1)} copy-done((bf16[32,2,16,512]{3,2,1,0:T(8,128)(2,1)S(1)}, bf16[32,2,16,512]{3,2,1,0:T(8,128)(2,1)}, u32[]{:S(2)}) %copy-start) | copy-done | bytes 1048600
  1.5 4.9 %collective-permute-start = (bf16[32,2,16,1]{3,0,2,1:T(8,128)(2,1)S(1)}, bf16[32,2,16,1]{3,0,2,1:T(8,128)(2,1)S(1)}, u32[]{:S(2)}, u32[]{:S(2)}) collective-permute-start(bf16[32,2,16,1]{3,0,2,1:T(8,128)(2,1)S(1)} %get-tuple-element.39), channel_id=1, source_target_pairs={{0,1},{1,2},{2,3},{4,5},{5,6},{6,7},{8,9},{9,10},{10,11},{12,13},{... | collective-permute-start | bytes 6152 | tf_op jit(solution)/shard_map/ppermute | solution.py:22
  6.5 1.3 %collective-permute-start.1 = (bf16[32,2,16,1]{3,0,2,1:T(8,128)(2,1)S(1)}, bf16[32,2,16,1]{3,0,2,1:T(8,128)(2,1)S(1)}, u32[]{:S(2)}, u32[]{:S(2)}) collective-permute-start(bf16[32,2,16,1]{3,0,2,1:T(8,128)(2,1)S(1)} %get-tuple-element.40), channel_id=1, source_target_pairs={{1,0},{2,1},{3,2},{5,4},{6,5},{7,6},{9,8},{10,9},{11,10},{13,12},{... | collective-permute-start | bytes 6152 | tf_op jit(solution)/shard_map/ppermute | solution.py:23
  7.8 4.2 %collective-permute-done = bf16[32,2,16,1]{3,0,2,1:T(8,128)(2,1)S(1)} collective-permute-done((bf16[32,2,16,1]{3,0,2,1:T(8,128)(2,1)S(1)}, bf16[32,2,16,1]{3,0,2,1:T(8,128)(2,1)S(1)}, u32[]{:S(2)}, u32[]{:S(2)}) %collective-permute-start) | collective-permute-done | bytes 2080 | tf_op jit(solution)/shard_map/ppermute | solution.py:22
  12.0 4.1 %collective-permute-done.1 = bf16[32,2,16,1]{3,0,2,1:T(8,128)(2,1)S(1)} collective-permute-done((bf16[32,2,16,1]{3,0,2,1:T(8,128)(2,1)S(1)}, bf16[32,2,16,1]{3,0,2,1:T(8,128)(2,1)S(1)}, u32[]{:S(2)}, u32[]{:S(2)}) %collective-permute-start.1) | collective-permute-done | bytes 2080 | tf_op jit(solution)/shard_map/ppermute | solution.py:23
  16.3 15.9 %all_gather.6 = bf16[3,3,3,64,32]{4,3,2,1,0:T(8,128)(2,1)S(1)} all-gather(bf16[3,3,3,16,32]{4,3,2,1,0:T(8,128)(2,1)S(1)} %copy-done.7), channel_id=1, replica_groups=mesh['space'=8,'chan'=4] {'chan'}, dimensions={3}, use_global_device_ids=true | all-gather | bytes 138240 | tf_op jit(solution)/shard_map/all_gather | solution.py:104
  32.5 1.6 %collective-permute-done.3 = bf16[32,2,1,130]{3,0,2,1:T(8,128)(2,1)S(1)} collective-permute-done((bf16[32,2,1,130]{3,0,2,1:T(8,128)(2,1)S(1)}, bf16[32,2,1,130]{3,0,2,1:T(8,128)(2,1)S(1)}, u32[]{:S(2)}, u32[]{:S(2)}) %collective-permute-start.3) | collective-permute-done | bytes 16672 | tf_op jit(solution)/shard_map/ppermute | solution.py:12
  35.2 0.9 copy.79
  36.1 0.9 copy.77
  37.0 0.9 copy.75
  42.9 1.5 %collective-permute-start.6 = (bf16[64,2,16,1]{3,0,2,1:T(8,128)(2,1)S(1)}, bf16[64,2,16,1]{3,0,2,1:T(8,128)(2,1)S(1)}, u32[]{:S(2)}, u32[]{:S(2)}) collective-permute-start(bf16[64,2,16,1]{3,0,2,1:T(8,128)(2,1)S(1)} %get-tuple-element.19), channel_id=1, source_target_pairs={{0,1},{1,2},{2,3},{4,5},{5,6},{6,7},{8,9},{9,10},{10,11},{12,13},{... | collective-permute-start | bytes 12296 | tf_op jit(solution)/shard_map/ppermute | solution.py:22
  44.4 1.3 %collective-permute-start.7 = (bf16[64,2,16,1]{3,0,2,1:T(8,128)(2,1)S(1)}, bf16[64,2,16,1]{3,0,2,1:T(8,128)(2,1)S(1)}, u32[]{:S(2)}, u32[]{:S(2)}) collective-permute-start(bf16[64,2,16,1]{3,0,2,1:T(8,128)(2,1)S(1)} %get-tuple-element.20), channel_id=1, source_target_pairs={{1,0},{2,1},{3,2},{5,4},{6,5},{7,6},{9,8},{10,9},{11,10},{13,12},{... | collective-permute-start | bytes 12296 | tf_op jit(solution)/shard_map/ppermute | solution.py:23
  45.7 10.6 %collective-permute-done.6 = bf16[64,2,16,1]{3,0,2,1:T(8,128)(2,1)S(1)} collective-permute-done((bf16[64,2,16,1]{3,0,2,1:T(8,128)(2,1)S(1)}, bf16[64,2,16,1]{3,0,2,1:T(8,128)(2,1)S(1)}, u32[]{:S(2)}, u32[]{:S(2)}) %collective-permute-start.6) | collective-permute-done | bytes 4128 | tf_op jit(solution)/shard_map/ppermute | solution.py:22
  56.4 4.6 %collective-permute-done.7 = bf16[64,2,16,1]{3,0,2,1:T(8,128)(2,1)S(1)} collective-permute-done((bf16[64,2,16,1]{3,0,2,1:T(8,128)(2,1)S(1)}, bf16[64,2,16,1]{3,0,2,1:T(8,128)(2,1)S(1)}, u32[]{:S(2)}, u32[]{:S(2)}) %collective-permute-start.7) | collective-permute-done | bytes 4128 | tf_op jit(solution)/shard_map/ppermute | solution.py:23
  61.3 2.5 %collective-permute-start.9 = (bf16[64,2,1,130]{3,0,2,1:T(8,128)(2,1)S(1)}, bf16[64,2,1,130]{3,0,2,1:T(8,128)(2,1)S(1)}, u32[]{:S(2)}, u32[]{:S(2)}) collective-permute-start(bf16[64,2,1,130]{3,0,2,1:T(8,128)(2,1)S(1)} %get-tuple-element.9), channel_id=1, source_target_pairs={{0,28},{4,0},{8,4},{12,8},{16,12},{20,16},{24,20},{28,24},{1,29},{... | collective-permute-start | bytes 99848 | tf_op jit(solution)/shard_map/ppermute | solution.py:12
  63.8 1.9 %collective-permute-done.8 = bf16[64,2,1,130]{3,0,2,1:T(8,128)(2,1)S(1)} collective-permute-done((bf16[64,2,1,130]{3,0,2,1:T(8,128)(2,1)S(1)}, bf16[64,2,1,130]{3,0,2,1:T(8,128)(2,1)S(1)}, u32[]{:S(2)}, u32[]{:S(2)}) %collective-permute-start.8) | collective-permute-done | bytes 33312 | tf_op jit(solution)/shard_map/ppermute | solution.py:12
  66.5 1.1 fusion.15
  67.6 5.3 %collective-permute-start.10 = (bf16[64,1,18,130]{3,0,2,1:T(8,128)(2,1)}, bf16[64,1,18,130]{3,0,2,1:T(8,128)(2,1)}, u32[]{:S(2)}, u32[]{:S(2)}) collective-permute-start(bf16[64,1,18,130]{3,0,2,1:T(8,128)(2,1)} %get-tuple-element.10), channel_id=1, source_target_pairs={{0,0},{4,4},{8,8},{12,12},{16,16},{20,20},{24,24},{28,28},{1,1},{5... | collective-permute-start | bytes 898568 | tf_op jit(solution)/shard_map/ppermute | solution.py:12
  72.9 15.3 %all_gather.7 = bf16[3,3,3,64,64]{4,3,2,1,0:T(8,128)(2,1)S(1)} all-gather(bf16[3,3,3,16,64]{4,3,2,1,0:T(8,128)(2,1)S(1)} %copy-done.8), channel_id=1, replica_groups=mesh['space'=8,'chan'=4] {'chan'}, dimensions={3}, use_global_device_ids=true | all-gather | bytes 276480 | tf_op jit(solution)/shard_map/all_gather | solution.py:105
  88.2 1.1 collective-permute-start.11
  89.3 0.7 slice_bitcast_fusion.8
  90.0 1.5 %copy.81 = bf16[64,3,64]{0,2,1:T(8,128)(2,1)} copy(bf16[64,3,64]{2,0,1:T(8,128)(2,1)} %get-tuple-element.21) | data formatting | bytes 49152 | tf_op jit(solution)/shard_map/transpose | solution.py:87
  91.5 1.5 %copy.97 = bf16[64,3,64]{0,2,1:T(8,128)(2,1)} copy(bf16[64,3,64]{2,0,1:T(8,128)(2,1)} %get-tuple-element.22) | data formatting | bytes 49152 | tf_op jit(solution)/shard_map/transpose | solution.py:87
  93.0 1.5 %copy.95 = bf16[64,3,64]{0,2,1:T(8,128)(2,1)} copy(bf16[64,3,64]{2,0,1:T(8,128)(2,1)} %get-tuple-element.23) | data formatting | bytes 49152 | tf_op jit(solution)/shard_map/transpose | solution.py:87
  94.5 1.5 %copy.93 = bf16[64,3,64]{0,2,1:T(8,128)(2,1)} copy(bf16[64,3,64]{2,0,1:T(8,128)(2,1)} %get-tuple-element.24) | data formatting | bytes 49152 | tf_op jit(solution)/shard_map/transpose | solution.py:87
  96.0 1.5 %copy.91 = bf16[64,3,64]{0,2,1:T(8,128)(2,1)} copy(bf16[64,3,64]{2,0,1:T(8,128)(2,1)} %get-tuple-element.25) | data formatting | bytes 49152 | tf_op jit(solution)/shard_map/transpose | solution.py:87
  97.5 0.7 copy.89
  98.7 1.2 pad_maximum_fusion.1
  99.9 0.9 fusion.14
  105.3 0.9 fusion.11
  106.6 14.4 %all_to_all.18 = bf16[64,2,16,128]{3,2,1,0:T(8,128)(2,1)S(1)} all-to-all(bf16[64,2,16,128]{3,2,1,0:T(8,128)(2,1)S(1)} %copy.99), channel_id=1, replica_groups=mesh['space'=8,'chan'=4] {'chan'}, dimensions={0} | all-to-all | bytes 1048576 | tf_op jit(solution)/shard_map/all_to_all | solution.py:117
  121.0 0.9 copy.140
  (76 shorter events, 12.7 us)
Async XLA Ops:
  0.0 1.2 %copy-start = (bf16[32,2,16,512]{3,2,1,0:T(8,128)(2,1)S(1)}, bf16[32,2,16,512]{3,2,1,0:T(8,128)(2,1)}, u32[]{:S(2)}) copy-start(bf16[32,2,16,512]{3,2,1,0:T(8,128)(2,1)} %param.3) | copy-start | bytes 3145732
  0.0 16.3 %copy-start.7 = (bf16[3,3,3,16,32]{4,3,2,1,0:T(8,128)(2,1)S(1)}, bf16[3,3,3,16,32]{4,3,2,1,0:T(8,128)(2,1)}, u32[]{:S(2)}) copy-start(bf16[3,3,3,16,32]{4,3,2,1,0:T(8,128)(2,1)} %param.4) | copy-start | bytes 82948
  1.5 10.5 %collective-permute-start = (bf16[32,2,16,1]{3,0,2,1:T(8,128)(2,1)S(1)}, bf16[32,2,16,1]{3,0,2,1:T(8,128)(2,1)S(1)}, u32[]{:S(2)}, u32[]{:S(2)}) collective-permute-start(bf16[32,2,16,1]{3,0,2,1:T(8,128)(2,1)S(1)} %get-tuple-element.39), channel_id=1, source_target_pairs={{0,1},{1,2},{2,3},{4,5},{5,6},{6,7},{8,9},{9,10},{10,11},{12,13},{... | collective-permute-start | bytes 6152 | tf_op jit(solution)/shard_map/ppermute | solution.py:22
  6.5 9.7 %collective-permute-start.1 = (bf16[32,2,16,1]{3,0,2,1:T(8,128)(2,1)S(1)}, bf16[32,2,16,1]{3,0,2,1:T(8,128)(2,1)S(1)}, u32[]{:S(2)}, u32[]{:S(2)}) collective-permute-start(bf16[32,2,16,1]{3,0,2,1:T(8,128)(2,1)S(1)} %get-tuple-element.40), channel_id=1, source_target_pairs={{1,0},{2,1},{3,2},{5,4},{6,5},{7,6},{9,8},{10,9},{11,10},{13,12},{... | collective-permute-start | bytes 6152 | tf_op jit(solution)/shard_map/ppermute | solution.py:23
  16.3 16.3 %collective-permute-start.2 = (bf16[32,2,1,130]{3,0,2,1:T(8,128)(2,1)S(1)}, bf16[32,2,1,130]{3,0,2,1:T(8,128)(2,1)S(1)}, u32[]{:S(2)}, u32[]{:S(2)}) collective-permute-start(bf16[32,2,1,130]{3,0,2,1:T(8,128)(2,1)S(1)} %get-tuple-element.15), channel_id=1, source_target_pairs={{0,4},{4,8},{8,12},{12,16},{16,20},{20,24},{24,28},{28,0},{1,5},{5... | collective-permute-start | bytes 49928 | tf_op jit(solution)/shard_map/ppermute | solution.py:12
  32.2 1.9 %collective-permute-start.3 = (bf16[32,2,1,130]{3,0,2,1:T(8,128)(2,1)S(1)}, bf16[32,2,1,130]{3,0,2,1:T(8,128)(2,1)S(1)}, u32[]{:S(2)}, u32[]{:S(2)}) collective-permute-start(bf16[32,2,1,130]{3,0,2,1:T(8,128)(2,1)S(1)} %get-tuple-element.16), channel_id=1, source_target_pairs={{0,28},{4,0},{8,4},{12,8},{16,12},{20,16},{24,20},{28,24},{1,29},{... | collective-permute-start | bytes 49928 | tf_op jit(solution)/shard_map/ppermute | solution.py:12
  34.5 4.0 %collective-permute-start.4 = (bf16[32,1,18,130]{3,0,2,1:T(8,128)(2,1)S(1)}, bf16[32,1,18,130]{3,0,2,1:T(8,128)(2,1)S(1)}, u32[]{:S(2)}, u32[]{:S(2)}) collective-permute-start(bf16[32,1,18,130]{3,0,2,1:T(8,128)(2,1)S(1)} %get-tuple-element.17), channel_id=1, source_target_pairs={{0,0},{4,4},{8,8},{12,12},{16,16},{20,20},{24,24},{28,28},{1,1},{5... | collective-permute-start | bytes 449288 | tf_op jit(solution)/shard_map/ppermute | solution.py:12
  38.4 0.1 collective-permute-start.5
  42.9 13.5 %collective-permute-start.6 = (bf16[64,2,16,1]{3,0,2,1:T(8,128)(2,1)S(1)}, bf16[64,2,16,1]{3,0,2,1:T(8,128)(2,1)S(1)}, u32[]{:S(2)}, u32[]{:S(2)}) collective-permute-start(bf16[64,2,16,1]{3,0,2,1:T(8,128)(2,1)S(1)} %get-tuple-element.19), channel_id=1, source_target_pairs={{0,1},{1,2},{2,3},{4,5},{5,6},{6,7},{8,9},{9,10},{10,11},{12,13},{... | collective-permute-start | bytes 12296 | tf_op jit(solution)/shard_map/ppermute | solution.py:22
  44.4 16.6 %collective-permute-start.7 = (bf16[64,2,16,1]{3,0,2,1:T(8,128)(2,1)S(1)}, bf16[64,2,16,1]{3,0,2,1:T(8,128)(2,1)S(1)}, u32[]{:S(2)}, u32[]{:S(2)}) collective-permute-start(bf16[64,2,16,1]{3,0,2,1:T(8,128)(2,1)S(1)} %get-tuple-element.20), channel_id=1, source_target_pairs={{1,0},{2,1},{3,2},{5,4},{6,5},{7,6},{9,8},{10,9},{11,10},{13,12},{... | collective-permute-start | bytes 12296 | tf_op jit(solution)/shard_map/ppermute | solution.py:23
  61.1 4.6 %collective-permute-start.8 = (bf16[64,2,1,130]{3,0,2,1:T(8,128)(2,1)S(1)}, bf16[64,2,1,130]{3,0,2,1:T(8,128)(2,1)S(1)}, u32[]{:S(2)}, u32[]{:S(2)}) collective-permute-start(bf16[64,2,1,130]{3,0,2,1:T(8,128)(2,1)S(1)} %get-tuple-element.8), channel_id=1, source_target_pairs={{0,4},{4,8},{8,12},{12,16},{16,20},{20,24},{24,28},{28,0},{1,5},{5... | collective-permute-start | bytes 99848 | tf_op jit(solution)/shard_map/ppermute | solution.py:12
  61.3 4.5 %collective-permute-start.9 = (bf16[64,2,1,130]{3,0,2,1:T(8,128)(2,1)S(1)}, bf16[64,2,1,130]{3,0,2,1:T(8,128)(2,1)S(1)}, u32[]{:S(2)}, u32[]{:S(2)}) collective-permute-start(bf16[64,2,1,130]{3,0,2,1:T(8,128)(2,1)S(1)} %get-tuple-element.9), channel_id=1, source_target_pairs={{0,28},{4,0},{8,4},{12,8},{16,12},{20,16},{24,20},{28,24},{1,29},{... | collective-permute-start | bytes 99848 | tf_op jit(solution)/shard_map/ppermute | solution.py:12
  65.8 7.1 %copy-start.8 = (bf16[3,3,3,16,64]{4,3,2,1,0:T(8,128)(2,1)S(1)}, bf16[3,3,3,16,64]{4,3,2,1,0:T(8,128)(2,1)}, u32[]{:S(2)}) copy-start(bf16[3,3,3,16,64]{4,3,2,1,0:T(8,128)(2,1)} %param.5) | copy-start | bytes 165892
  67.6 31.0 %collective-permute-start.10 = (bf16[64,1,18,130]{3,0,2,1:T(8,128)(2,1)}, bf16[64,1,18,130]{3,0,2,1:T(8,128)(2,1)}, u32[]{:S(2)}, u32[]{:S(2)}) collective-permute-start(bf16[64,1,18,130]{3,0,2,1:T(8,128)(2,1)} %get-tuple-element.10), channel_id=1, source_target_pairs={{0,0},{4,4},{8,8},{12,12},{16,16},{20,20},{24,24},{28,28},{1,1},{5... | collective-permute-start | bytes 898568 | tf_op jit(solution)/shard_map/ppermute | solution.py:12
  88.2 10.4 %collective-permute-start.11 = (bf16[64,1,18,130]{3,0,2,1:T(8,128)(2,1)}, bf16[64,1,18,130]{3,0,2,1:T(8,128)(2,1)S(1)}, u32[]{:S(2)}, u32[]{:S(2)}) collective-permute-start(bf16[64,1,18,130]{3,0,2,1:T(8,128)(2,1)} %get-tuple-element.11), channel_id=1, source_target_pairs={{0,0},{4,4},{8,8},{12,12},{16,16},{20,20},{24,24},{28,28},{1,1},{5... | collective-permute-start | bytes 898568 | tf_op jit(solution)/shard_map/ppermute | solution.py:12
  100.8 0.8 copy-start.1
  101.1 0.9 copy-start.2
  101.6 0.9 copy-start.3
  102.1 0.9 copy-start.4
  102.6 0.9 copy-start.5
  104.4 0.9 copy-start.6
where the time goes:
time: 124 us; the launch traced here: 122 us
  blocking collectives  45.7 us (37%)
  waiting for transfers between devices  27.2 us (22%)
  local copies, waits for them, and re-layouts  19.2 us (15%)
  starting transfers between devices  18.5 us (15%)
  matrix products  7.62 us (6%)
  other arithmetic  3.28 us (3%)
    all_gather x1, blocking collectives, local(): lax.all_gather(first_filters, 'chan', axis=3, tiled=True)  15.9 us
    all_gather x1, blocking collectives, local(): lax.all_gather(second_filters, 'chan', axis=3, tiled=True)  15.3 us
    ppermute x2, waiting for transfers between devices, extended(): before = lax.ppermute(last, axis, up)  14.9 us
    all_to_all x1, blocking collectives, local(): lax.all_to_all(result, 'chan', split_axis=0, concat_axis=3, tiled=True)  14.4 us
    transpose x20, local copies, waits for them, and re-layouts, correlate(): filters[depth_tap, height_tap].transpose(1, 0, 2).reshape(out_count, -1)  13.1 us
    ppermute x8, starting transfers between devices, passed_along(): return lax.ppermute(value, axis, pairs)  9.47 us
    ppermute x2, waiting for transfers between devices, extended(): after = lax.ppermute(initial, axis, down)  8.75 us
    dot_general x18, matrix products, correlate(): jnp.einsum('ok,kdhw->odhw', matrix, window, preferred_element_type=jnp.fl...  7.62 us
  transfers between devices with their start and end apart: 12, of which 6 were waited for; matrix products, arithmetic and copies ran while one was open for 11% of the time, Pallas kernels for 0%

commit v1 on v0

--- a/solution.py
+++ b/solution.py
@@ -1,6 +1,10 @@
+import functools
+
 import jax
 import jax.numpy as jnp
 from jax import lax
+from jax.experimental import pallas as pl
+from jax.experimental.pallas import tpu as pltpu
 from jax.sharding import PartitionSpec as P
 
 GH = 8
@@ -117,9 +121,203 @@
     return lax.all_to_all(result, "chan", split_axis=0, concat_axis=3, tiled=True)
 
 
+MESH = pl.DeviceIdType.MESH
+BF = jnp.bfloat16
+F32 = jnp.float32
+LANES = 128
+
+
+def combine_width(product, part):
+    lane = lax.broadcasted_iota(jnp.int32, (part, product.shape[1]), 1)
+    width = product.shape[1]
+    left = jnp.where(lane == 0, 0.0, pltpu.roll(product[:part], 1, 1))
+    right = jnp.where(lane == width - 1, 0.0, pltpu.roll(product[2 * part :], width - 1, 1))
+    return left + product[part : 2 * part] + right
+
+
+def tile_kernel(
+    sizes, vox_hbm, first_hbm, second_hbm, out_ref,
+    vox, first, second, wide, xs, gathered, w1, w2, hid, rows_out,
+    load_sem, send_sem, recv_sem,
+):
+    n_space, n_chan, c_in, own, c_mid, height, width = sizes
+    s = lax.axis_index("space")
+    c = lax.axis_index("chan")
+    below, above = lax.rem(s + 1, n_space), lax.rem(s + n_space - 1, n_space)
+    position = lax.rem(s + GH + GH // 4, n_space)
+
+    loads = [
+        pltpu.make_async_copy(first_hbm, first, load_sem.at[0]),
+        pltpu.make_async_copy(vox_hbm, vox, load_sem.at[1]),
+        pltpu.make_async_copy(second_hbm, second, load_sem.at[2]),
+    ]
+    for load in loads:
+        load.start()
+
+    barrier = pltpu.get_barrier_semaphore()
+    for neighbour in (below, above):
+        pl.semaphore_signal(barrier, inc=1, device_id={"space": neighbour}, device_id_type=MESH)
+    for k in range(1, n_chan):
+        pl.semaphore_signal(
+            barrier, inc=1, device_id={"chan": lax.rem(c + k, n_chan)}, device_id_type=MESH
+        )
+
+    loads[0].wait()
+    spare = jnp.zeros((own, c_in), BF)
+    for e in range(3):
+        for a in range(3):
+            gathered[c, e * 3 + a] = jnp.concatenate(
+                [first[a, 0, e], first[a, 1, e], first[a, 2, e], spare], axis=1
+            )
+    pl.semaphore_wait(barrier, n_chan + 1)
+    copies = []
+    for k in range(1, n_chan):
+        copy = pltpu.make_async_remote_copy(
+            src_ref=gathered.at[c],
+            dst_ref=gathered.at[c],
+            send_sem=send_sem.at[k - 1],
+            recv_sem=recv_sem.at[k - 1],
+            device_id={"chan": lax.rem(c + k, n_chan)},
+            device_id_type=MESH,
+        )
+        copy.start()
+        copies.append(copy)
+
+    loads[1].wait()
+    tiles = width // LANES
+    for d in range(2):
+        for t in range(tiles):
+            part = vox[:, d, :, pl.ds(t * LANES, LANES)].astype(F32)
+            wide[d, t] = part.reshape(c_in * height, LANES)
+
+    def turn(h):
+        for d in range(2):
+            for t in range(tiles):
+                xs[d, pl.ds((h + 2) * c_in, c_in), pl.ds(t * LANES, LANES)] = wide[
+                    d, t, pl.ds(h, c_in, stride=height), :
+                ].astype(BF)
+
+    for h in (0, 1, height - 2, height - 1):
+        turn(h)
+    halos = []
+    for i, (start, landing, target) in enumerate(
+        ((height, 0, below), (2, height + 2, above))
+    ):
+        copy = pltpu.make_async_remote_copy(
+            src_ref=xs.at[:, pl.ds(start * c_in, 2 * c_in), :],
+            dst_ref=xs.at[:, pl.ds(landing * c_in, 2 * c_in), :],
+            send_sem=send_sem.at[n_chan - 1 + i],
+            recv_sem=recv_sem.at[n_chan - 1 + i],
+            device_id={"space": target},
+            device_id_type=MESH,
+        )
+        copy.start()
+        halos.append(copy)
+    for h in range(2, height - 2):
+        turn(h)
+    xs[:, pl.ds((height + 4) * c_in, c_in), :] = jnp.zeros((2, c_in, width), BF)
+
+    loads[2].wait()
+    for e in range(3):
+        for od in range(2):
+            w2[pl.ds((e * 2 + od) * own, own), :] = jnp.concatenate(
+                [second[i - od + 1, b, e] for b in range(3) for i in range(2)], axis=1
+            )
+
+    for copy in copies:
+        copy.wait()
+    lanes = 4 * c_in
+    for e in range(3):
+        for od in range(2):
+            for k in range(n_chan):
+                at = pl.ds((e * 2 + od) * c_mid + k * own, own)
+                for i in range(2):
+                    w1[at, pl.ds(i * lanes, lanes)] = gathered[k, e * 3 + i - od + 1]
+
+    def layer_one(r, _=None):
+        window = pl.ds(pl.multiple_of(r * c_in, c_in), lanes)
+        stacked = jnp.concatenate([xs[0, window, :], xs[1, window, :]], axis=0)
+        product = jnp.dot(w1[...], stacked, preferred_element_type=F32)
+        row = jnp.maximum(combine_width(product, 2 * c_mid), 0.0).astype(BF)
+        hid[pl.ds(pl.multiple_of(r * 2 * c_mid, 2 * c_mid), 2 * c_mid), :] = row
+
+    lax.fori_loop(2, height - 1, lambda r, _: layer_one(r), None)
+    for copy in halos:
+        copy.wait()
+
+    @pl.when(position == 0)
+    def _():
+        xs[:, : 2 * c_in, :] = jnp.zeros((2, 2 * c_in, width), BF)
+
+    @pl.when(position == n_space - 1)
+    def _():
+        xs[:, pl.ds((height + 2) * c_in, 2 * c_in), :] = jnp.zeros((2, 2 * c_in, width), BF)
+
+    lax.fori_loop(0, 2, lambda r, _: layer_one(r), None)
+    lax.fori_loop(height - 1, height + 2, lambda r, _: layer_one(r), None)
+
+    @pl.when(position == 0)
+    def _():
+        hid[: 2 * c_mid, :] = jnp.zeros((2 * c_mid, width), BF)
+
+    @pl.when(position == n_space - 1)
+    def _():
+        hid[pl.ds((height + 1) * 2 * c_mid, 2 * c_mid), :] = jnp.zeros((2 * c_mid, width), BF)
+
+    def layer_two(r):
+        window = pl.ds(pl.multiple_of(r * 2 * c_mid, 2 * c_mid), 6 * c_mid)
+        product = jnp.dot(w2[...], hid[window, :], preferred_element_type=F32)
+        row = jnp.maximum(combine_width(product, 2 * own), 0.0)
+        for d in range(2):
+            for t in range(tiles):
+                rows_out[d, t, pl.ds(pl.multiple_of(r * own, own), own), :] = row[
+                    d * own : (d + 1) * own, t * LANES : (t + 1) * LANES
+                ]
+
+    lax.fori_loop(0, height, lambda r, _: layer_two(r), None)
+    for d in range(2):
+        for o in range(own):
+            for t in range(tiles):
+                out_ref[o, d, :, pl.ds(t * LANES, LANES)] = rows_out[
+                    d, t, pl.ds(o, height, stride=own), :
+                ].astype(BF)
+
+
+def one_layer_of_tiles(voxels, first_filters, second_filters):
+    n_space, n_chan = lax.axis_size("space"), lax.axis_size("chan")
+    c_in, depth, height, width = voxels.shape
+    own, c_mid = second_filters.shape[3:]
+    sizes = (n_space, n_chan, c_in, own, c_mid, height, width)
+    any_space = pl.BlockSpec(memory_space=pl.ANY)
+    return pl.pallas_call(
+        functools.partial(tile_kernel, sizes),
+        out_shape=jax.ShapeDtypeStruct((own, depth, height, width), BF),
+        in_specs=[any_space] * 3,
+        out_specs=pl.BlockSpec(memory_space=pltpu.VMEM),
+        scratch_shapes=[
+            pltpu.VMEM(voxels.shape, BF),
+            pltpu.VMEM(first_filters.shape, BF),
+            pltpu.VMEM(second_filters.shape, BF),
+            pltpu.VMEM((2, width // LANES, c_in * height, LANES), F32),
+            pltpu.VMEM((2, (height + 5) * c_in, width), BF),
+            pltpu.VMEM((n_chan, 9, own, 4 * c_in), BF),
+            pltpu.VMEM((6 * c_mid, 8 * c_in), BF),
+            pltpu.VMEM((6 * own, 6 * c_mid), BF),
+            pltpu.VMEM(((height + 2) * 2 * c_mid, width), BF),
+            pltpu.VMEM((2, width // LANES, height * own, LANES), F32),
+            pltpu.SemaphoreType.DMA((3,)),
+            pltpu.SemaphoreType.DMA((n_chan + 1,)),
+            pltpu.SemaphoreType.DMA((n_chan + 1,)),
+        ],
+        compiler_params=pltpu.CompilerParams(
+            collective_id=0, has_side_effects=True, vmem_limit_bytes=32 * 1024 * 1024
+        ),
+    )(voxels, first_filters, second_filters)
+
+
 def solution(mesh):
     return jax.shard_map(
-        local,
+        one_layer_of_tiles if mesh.shape["space"] == GH else local,
         mesh=mesh,
         in_specs=(
             P(None, "space", None, None),

time: 124 us -> 25.3 us (0.20); the launches traced: 122 us -> 25.1 us
  blocking collectives: 45.7 us -> 0 us
  waiting for transfers between devices: 27.2 us -> 0 us
  Pallas kernels: 0 us -> 21.3 us
  starting transfers between devices: 18.5 us -> 0 us
  local copies, waits for them, and re-layouts: 19.2 us -> 3.81 us
  matrix products: 7.62 us -> 0 us
  other arithmetic: 3.28 us -> 0 us
    all_gather x2 -> x0, blocking collectives: 31.2 us -> none  [the longest x1 15.9 us: local(): lax.all_gather(first_filters, 'chan', axis=3, tiled=True)]
    ppermute x12 -> x0, waiting for transfers between devices: 27.2 us -> none  [the longest x2 14.9 us: extended(): before = lax.ppermute(last, axis, up)]
    pallas_call x0 -> x1, Pallas kernels: none -> 21.3 us  [one_layer_of_tiles(): pl.pallas_call(functools.partial(tile_kernel, sizes), out_shape=jax.Shape...]
    ppermute x12 -> x0, starting transfers between devices: 18.5 us -> none  [the longest x8 9.47 us: passed_along(): return lax.ppermute(value, axis, pairs)]
    all_to_all x1 -> x0, blocking collectives: 14.4 us -> none  [local(): lax.all_to_all(result, 'chan', split_axis=0, concat_axis=3, tiled=True)]
    transpose x20 -> x0, local copies, waits for them, and re-layouts: 13.1 us -> none  [correlate(): filters[depth_tap, height_tap].transpose(1, 0, 2).reshape(out_count, -1)]
    dot_general x18 -> x0, matrix products: 7.62 us -> none  [correlate(): jnp.einsum('ok,kdhw->odhw', matrix, window, preferred_element_type=jnp.fl...]
    slice x6 -> x0, local copies, waits for them, and re-layouts: 2.92 us -> none  [the longest x2 1.38 us: stack_taps(): sided[..., :-2]]
  transfers between devices with their start and end apart: 12 -> 0, of which waited for: 6 -> 0; matrix products, arithmetic and copies ran while one was open for 11% -> 0% of each run, Pallas kernels for 0% -> 0%
where the time goes in v1:
time: 25.3 us; the launch traced here: 25.1 us
  Pallas kernels  21.3 us (84%)
  local copies, waits for them, and re-layouts  3.81 us (15%)
    pallas_call x1, Pallas kernels, one_layer_of_tiles(): pl.pallas_call(functools.partial(tile_kernel, sizes), out_shape=jax.Shape...  21.3 us
    unnamed x7, local copies, waits for them, and re-layouts  3.81 us

profile of v1, /device:TPU:0, one launch (start us, length us, event | category | flops | bytes accessed | tf_op | source)
XLA Modules:
  0.0 25.1 jit_solution(13116937776029086674)
XLA Ops:
  0.0 0.0 copy-start
  0.0 1.2 %copy-done = bf16[32,2,16,512]{3,2,1,0:T(8,128)(2,1)S(1)} copy-done((bf16[32,2,16,512]{3,2,1,0:T(8,128)(2,1)S(1)}, bf16[32,2,16,512]{3,2,1,0:T(8,128)(2,1)}, u32[]{:S(2)}) %copy-start) | copy-done | bytes 1048600
  1.2 0.0 copy-start.1
  1.2 0.9 %copy-done.1 = bf16[3,3,3,16,32]{4,3,2,1,0:T(8,128)(2,1)S(1)} copy-done((bf16[3,3,3,16,32]{4,3,2,1,0:T(8,128)(2,1)S(1)}, bf16[3,3,3,16,32]{4,3,2,1,0:T(8,128)(2,1)}, u32[]{:S(2)}) %copy-start.1) | copy-done | bytes 27672
  2.1 0.0 copy-start.2
  2.1 0.9 %copy-done.2 = bf16[3,3,3,16,64]{4,3,2,1,0:T(8,128)(2,1)S(1)} copy-done((bf16[3,3,3,16,64]{4,3,2,1,0:T(8,128)(2,1)S(1)}, bf16[3,3,3,16,64]{4,3,2,1,0:T(8,128)(2,1)}, u32[]{:S(2)}) %copy-start.2) | copy-done | bytes 55320
  3.0 21.3 %shard_map.37 = bf16[16,2,16,512]{3,2,1,0:T(8,128)(2,1)S(1)} custom-call(bf16[32,2,16,512]{3,2,1,0:T(8,128)(2,1)S(1)} %copy-done, bf16[3,3,3,16,32]{4,3,2,1,0:T(8,128)(2,1)S(1)} %copy-done.1, bf16[3,3,3,16,64]{4,3,2,1,0:T(8,128)(2,1)S(1)} %copy-done.2), custom_call_target="tpu_custom_call" | custom-call | tf_op jit(solution)/shard_map/pallas_call | solution.py:292
  24.3 0.8 %copy.5 = bf16[16,2,16,512]{3,2,1,0:T(8,128)(2,1)} copy(bf16[16,2,16,512]{3,2,1,0:T(8,128)(2,1)S(1)} %shard_map.37) | data formatting | bytes 1048576
Async XLA Ops:
  0.0 1.2 %copy-start = (bf16[32,2,16,512]{3,2,1,0:T(8,128)(2,1)S(1)}, bf16[32,2,16,512]{3,2,1,0:T(8,128)(2,1)}, u32[]{:S(2)}) copy-start(bf16[32,2,16,512]{3,2,1,0:T(8,128)(2,1)} %vox_hbm.1) | copy-start | bytes 3145732
  1.2 0.9 %copy-start.1 = (bf16[3,3,3,16,32]{4,3,2,1,0:T(8,128)(2,1)S(1)}, bf16[3,3,3,16,32]{4,3,2,1,0:T(8,128)(2,1)}, u32[]{:S(2)}) copy-start(bf16[3,3,3,16,32]{4,3,2,1,0:T(8,128)(2,1)} %first_hbm.1) | copy-start | bytes 82948
  2.1 0.9 %copy-start.2 = (bf16[3,3,3,16,64]{4,3,2,1,0:T(8,128)(2,1)S(1)}, bf16[3,3,3,16,64]{4,3,2,1,0:T(8,128)(2,1)}, u32[]{:S(2)}) copy-start(bf16[3,3,3,16,64]{4,3,2,1,0:T(8,128)(2,1)} %second_hbm.1) | copy-start | bytes 165892

commit v2 on v1

--- a/solution.py
+++ b/solution.py
@@ -169,6 +169,23 @@
             gathered[c, e * 3 + a] = jnp.concatenate(
                 [first[a, 0, e], first[a, 1, e], first[a, 2, e], spare], axis=1
             )
+    loads[1].wait()
+    tiles = width // LANES
+    for d in range(2):
+        for t in range(tiles):
+            part = vox[:, d, :, pl.ds(t * LANES, LANES)].astype(F32)
+            wide[d, t] = part.reshape(c_in * height, LANES)
+
+    def turn(h):
+        for d in range(2):
+            for t in range(tiles):
+                xs[d, pl.ds((h + 2) * c_in, c_in), pl.ds(t * LANES, LANES)] = wide[
+                    d, t, pl.ds(h, c_in, stride=height), :
+                ].astype(BF)
+
+    for h in (0, 1, height - 2, height - 1):
+        turn(h)
+
     pl.semaphore_wait(barrier, n_chan + 1)
     copies = []
     for k in range(1, n_chan):
@@ -182,23 +199,6 @@
         )
         copy.start()
         copies.append(copy)
-
-    loads[1].wait()
-    tiles = width // LANES
-    for d in range(2):
-        for t in range(tiles):
-            part = vox[:, d, :, pl.ds(t * LANES, LANES)].astype(F32)
-            wide[d, t] = part.reshape(c_in * height, LANES)
-
-    def turn(h):
-        for d in range(2):
-            for t in range(tiles):
-                xs[d, pl.ds((h + 2) * c_in, c_in), pl.ds(t * LANES, LANES)] = wide[
-                    d, t, pl.ds(h, c_in, stride=height), :
-                ].astype(BF)
-
-    for h in (0, 1, height - 2, height - 1):
-        turn(h)
     halos = []
     for i, (start, landing, target) in enumerate(
         ((height, 0, below), (2, height + 2, above))
@@ -217,6 +217,32 @@
         turn(h)
     xs[:, pl.ds((height + 4) * c_in, c_in), :] = jnp.zeros((2, c_in, width), BF)
 
+    lanes = 4 * c_in
+
+    def lay_filters(k):
+        source = lax.rem(c + n_chan - k, n_chan)
+        for e in range(3):
+            for od in range(2):
+                at = pl.ds(k * 6 * own + (e * 2 + od) * own, own)
+                for i in range(2):
+                    w1[at, pl.ds(i * lanes, lanes)] = gathered[source, e * 3 + i - od + 1]
+
+    def layer_one(r, first_k, last_k):
+        window = pl.ds(pl.multiple_of(r * c_in, c_in), lanes)
+        stacked = jnp.concatenate([xs[0, window, :], xs[1, window, :]], axis=0)
+        matrix = w1[first_k * 6 * own : last_k * 6 * own]
+        product = jnp.dot(matrix, stacked, preferred_element_type=F32)
+        for k in range(first_k, last_k):
+            part = product[(k - first_k) * 6 * own : (k - first_k + 1) * 6 * own]
+            row = jnp.maximum(combine_width(part, 2 * own), 0.0).astype(BF)
+            source = lax.rem(c + n_chan - k, n_chan)
+            for od in range(2):
+                at = pl.multiple_of(r * 2 * c_mid + od * c_mid + source * own, own)
+                hid[pl.ds(at, own), :] = row[od * own : (od + 1) * own]
+
+    lay_filters(0)
+    lax.fori_loop(2, height - 1, lambda r, _: layer_one(r, 0, 1), None, unroll=4)
+
     loads[2].wait()
     for e in range(3):
         for od in range(2):
@@ -226,22 +252,9 @@
 
     for copy in copies:
         copy.wait()
-    lanes = 4 * c_in
-    for e in range(3):
-        for od in range(2):
-            for k in range(n_chan):
-                at = pl.ds((e * 2 + od) * c_mid + k * own, own)
-                for i in range(2):
-                    w1[at, pl.ds(i * lanes, lanes)] = gathered[k, e * 3 + i - od + 1]
-
-    def layer_one(r, _=None):
-        window = pl.ds(pl.multiple_of(r * c_in, c_in), lanes)
-        stacked = jnp.concatenate([xs[0, window, :], xs[1, window, :]], axis=0)
-        product = jnp.dot(w1[...], stacked, preferred_element_type=F32)
-        row = jnp.maximum(combine_width(product, 2 * c_mid), 0.0).astype(BF)
-        hid[pl.ds(pl.multiple_of(r * 2 * c_mid, 2 * c_mid), 2 * c_mid), :] = row
-
-    lax.fori_loop(2, height - 1, lambda r, _: layer_one(r), None)
+    for k in range(1, n_chan):
+        lay_filters(k)
+    lax.fori_loop(2, height - 1, lambda r, _: layer_one(r, 1, n_chan), None, unroll=2)
     for copy in halos:
         copy.wait()
 
@@ -253,8 +266,8 @@
     def _():
         xs[:, pl.ds((height + 2) * c_in, 2 * c_in), :] = jnp.zeros((2, 2 * c_in, width), BF)
 
-    lax.fori_loop(0, 2, lambda r, _: layer_one(r), None)
-    lax.fori_loop(height - 1, height + 2, lambda r, _: layer_one(r), None)
+    lax.fori_loop(0, 2, lambda r, _: layer_one(r, 0, n_chan), None, unroll=1)
+    lax.fori_loop(height - 1, height + 2, lambda r, _: layer_one(r, 0, n_chan), None, unroll=1)
 
     @pl.when(position == 0)
     def _():
@@ -274,7 +287,7 @@
                     d * own : (d + 1) * own, t * LANES : (t + 1) * LANES
                 ]
 
-    lax.fori_loop(0, height, lambda r, _: layer_two(r), None)
+    lax.fori_loop(0, height, lambda r, _: layer_two(r), None, unroll=4)
     for d in range(2):
         for o in range(own):
             for t in range(tiles):
@@ -310,7 +323,7 @@
             pltpu.SemaphoreType.DMA((n_chan + 1,)),
         ],
         compiler_params=pltpu.CompilerParams(
-            collective_id=0, has_side_effects=True, vmem_limit_bytes=32 * 1024 * 1024
+            collective_id=0, has_side_effects=True, vmem_limit_bytes=60 * 1024 * 1024
         ),
     )(voxels, first_filters, second_filters)
 

time: 25.3 us -> 19.3 us (0.76)
  Pallas kernels: 21.3 us -> 17.3 us
  local copies, waits for them, and re-layouts: 3.81 us -> 1.88 us
    pallas_call x1, Pallas kernels: 21.3 us -> 17.3 us  [one_layer_of_tiles(): pl.pallas_call(functools.partial(tile_kernel, sizes), out_shape=jax.Shape...]
    unnamed x7 -> x1, local copies, waits for them, and re-layouts: 3.81 us -> 1.88 us
where the time goes in v2:
time: 19.3 us; the launch traced here: 19.2 us
  Pallas kernels  17.3 us (90%)
  local copies, waits for them, and re-layouts  1.88 us (10%)
    pallas_call x1, Pallas kernels, one_layer_of_tiles(): pl.pallas_call(functools.partial(tile_kernel, sizes), out_shape=jax.Shape...  17.3 us
    unnamed x1, local copies, waits for them, and re-layouts  1.88 us

profile of v2, /device:TPU:0, one launch (start us, length us, event | category | flops | bytes accessed | tf_op | source)
XLA Modules:
  0.0 19.2 jit_solution(15249354121767122593)
XLA Ops:
  0.0 17.3 %shard_map.37 = bf16[16,2,16,512]{3,2,1,0:T(8,128)(2,1)} custom-call(bf16[32,2,16,512]{3,2,1,0:T(8,128)(2,1)} %vox_hbm.1, bf16[3,3,3,16,32]{4,3,2,1,0:T(8,128)(2,1)} %first_hbm.1, bf16[3,3,3,16,64]{4,3,2,1,0:T(8,128)(2,1)} %second_hbm.1), custom_call_target="tpu_custom_call" | custom-call | tf_op jit(solution)/shard_map/pallas_call | solution.py:305
  17.3 1.9 %copy.5 = bf16[16,2,16,512]{3,2,1,0:T(8,128)(2,1)} copy(bf16[16,2,16,512]{3,2,1,0:T(8,128)(2,1)} %shard_map.37) | data formatting | bytes 1048576

commit v3 on v2

--- a/solution.py
+++ b/solution.py
@@ -241,7 +241,7 @@
                 hid[pl.ds(at, own), :] = row[od * own : (od + 1) * own]
 
     lay_filters(0)
-    lax.fori_loop(2, height - 1, lambda r, _: layer_one(r, 0, 1), None, unroll=4)
+    lax.fori_loop(2, height - 1, lambda r, _: layer_one(r, 0, 1), None, unroll=13)
 
     loads[2].wait()
     for e in range(3):
@@ -254,7 +254,7 @@
         copy.wait()
     for k in range(1, n_chan):
         lay_filters(k)
-    lax.fori_loop(2, height - 1, lambda r, _: layer_one(r, 1, n_chan), None, unroll=2)
+    lax.fori_loop(2, height - 1, lambda r, _: layer_one(r, 1, n_chan), None, unroll=13)
     for copy in halos:
         copy.wait()
 
@@ -266,8 +266,8 @@
     def _():
         xs[:, pl.ds((height + 2) * c_in, 2 * c_in), :] = jnp.zeros((2, 2 * c_in, width), BF)
 
-    lax.fori_loop(0, 2, lambda r, _: layer_one(r, 0, n_chan), None, unroll=1)
-    lax.fori_loop(height - 1, height + 2, lambda r, _: layer_one(r, 0, n_chan), None, unroll=1)
+    lax.fori_loop(0, 2, lambda r, _: layer_one(r, 0, n_chan), None, unroll=3)
+    lax.fori_loop(height - 1, height + 2, lambda r, _: layer_one(r, 0, n_chan), None, unroll=3)
 
     @pl.when(position == 0)
     def _():
@@ -287,7 +287,7 @@
                     d * own : (d + 1) * own, t * LANES : (t + 1) * LANES
                 ]
 
-    lax.fori_loop(0, height, lambda r, _: layer_two(r), None, unroll=4)
+    lax.fori_loop(0, height, lambda r, _: layer_two(r), None, unroll=16)
     for d in range(2):
         for o in range(own):
             for t in range(tiles):

time: 19.3 us -> 16.9 us (0.88)
  Pallas kernels: 17.3 us -> 14.8 us
    pallas_call x1, Pallas kernels: 17.3 us -> 14.8 us  [one_layer_of_tiles(): pl.pallas_call(functools.partial(tile_kernel, sizes), out_shape=jax.Shape...]
where the time goes in v3:
time: 16.9 us; the launch traced here: 16.7 us
  Pallas kernels  14.8 us (88%)
  local copies, waits for them, and re-layouts  1.88 us (11%)
    pallas_call x1, Pallas kernels, one_layer_of_tiles(): pl.pallas_call(functools.partial(tile_kernel, sizes), out_shape=jax.Shape...  14.8 us
    unnamed x1, local copies, waits for them, and re-layouts  1.88 us

profile of v3, /device:TPU:0, one launch (start us, length us, event | category | flops | bytes accessed | tf_op | source)
XLA Modules:
  0.0 16.7 jit_solution(15868436296613010384)
XLA Ops:
  0.0 14.8 %shard_map.37 = bf16[16,2,16,512]{3,2,1,0:T(8,128)(2,1)} custom-call(bf16[32,2,16,512]{3,2,1,0:T(8,128)(2,1)} %vox_hbm.1, bf16[3,3,3,16,32]{4,3,2,1,0:T(8,128)(2,1)} %first_hbm.1, bf16[3,3,3,16,64]{4,3,2,1,0:T(8,128)(2,1)} %second_hbm.1), custom_call_target="tpu_custom_call" | custom-call | tf_op jit(solution)/shard_map/pallas_call | solution.py:305
  14.8 1.9 %copy.5 = bf16[16,2,16,512]{3,2,1,0:T(8,128)(2,1)} copy(bf16[16,2,16,512]{3,2,1,0:T(8,128)(2,1)} %shard_map.37) | data formatting | bytes 1048576

commit v4 on v3

--- a/solution.py
+++ b/solution.py
@@ -164,11 +164,9 @@
 
     loads[0].wait()
     spare = jnp.zeros((own, c_in), BF)
-    for e in range(3):
-        for a in range(3):
-            gathered[c, e * 3 + a] = jnp.concatenate(
-                [first[a, 0, e], first[a, 1, e], first[a, 2, e], spare], axis=1
-            )
+    pieces = [first[a, b, e] for e in range(3) for a in range(3) for b in range(3)]
+    gathered[c] = jnp.concatenate(pieces + [spare] * (-len(pieces) % (LANES // c_in)), axis=1)
+
     loads[1].wait()
     tiles = width // LANES
     for d in range(2):
@@ -221,11 +219,14 @@
 
     def lay_filters(k):
         source = lax.rem(c + n_chan - k, n_chan)
+        whole = gathered[source]
         for e in range(3):
             for od in range(2):
                 at = pl.ds(k * 6 * own + (e * 2 + od) * own, own)
                 for i in range(2):
-                    w1[at, pl.ds(i * lanes, lanes)] = gathered[source, e * 3 + i - od + 1]
+                    start = (e * 3 + i - od + 1) * 3 * c_in
+                    taps = whole[:, start : start + 3 * c_in]
+                    w1[at, pl.ds(i * lanes, lanes)] = jnp.concatenate([taps, spare], axis=1)
 
     def layer_one(r, first_k, last_k):
         window = pl.ds(pl.multiple_of(r * c_in, c_in), lanes)
@@ -258,24 +259,15 @@
     for copy in halos:
         copy.wait()
 
-    @pl.when(position == 0)
-    def _():
-        xs[:, : 2 * c_in, :] = jnp.zeros((2, 2 * c_in, width), BF)
-
-    @pl.when(position == n_space - 1)
-    def _():
-        xs[:, pl.ds((height + 2) * c_in, 2 * c_in), :] = jnp.zeros((2, 2 * c_in, width), BF)
-
+    for edge, start in ((0, 0), (n_space - 1, height + 2)):
+        at = pl.ds(start * c_in, 2 * c_in)
+        xs[:, at, :] = jnp.where(position == edge, jnp.zeros((), BF), xs[:, at, :])
     lax.fori_loop(0, 2, lambda r, _: layer_one(r, 0, n_chan), None, unroll=3)
     lax.fori_loop(height - 1, height + 2, lambda r, _: layer_one(r, 0, n_chan), None, unroll=3)
 
-    @pl.when(position == 0)
-    def _():
-        hid[: 2 * c_mid, :] = jnp.zeros((2 * c_mid, width), BF)
-
-    @pl.when(position == n_space - 1)
-    def _():
-        hid[pl.ds((height + 1) * 2 * c_mid, 2 * c_mid), :] = jnp.zeros((2 * c_mid, width), BF)
+    for edge, start in ((0, 0), (n_space - 1, height + 1)):
+        at = pl.ds(start * 2 * c_mid, 2 * c_mid)
+        hid[at, :] = jnp.where(position == edge, jnp.zeros((), BF), hid[at, :])
 
     def layer_two(r):
         window = pl.ds(pl.multiple_of(r * 2 * c_mid, 2 * c_mid), 6 * c_mid)
@@ -313,7 +305,7 @@
             pltpu.VMEM(second_filters.shape, BF),
             pltpu.VMEM((2, width // LANES, c_in * height, LANES), F32),
             pltpu.VMEM((2, (height + 5) * c_in, width), BF),
-            pltpu.VMEM((n_chan, 9, own, 4 * c_in), BF),
+            pltpu.VMEM((n_chan, own, pl.cdiv(27 * c_in, LANES) * LANES), BF),
             pltpu.VMEM((6 * c_mid, 8 * c_in), BF),
             pltpu.VMEM((6 * own, 6 * c_mid), BF),
             pltpu.VMEM(((height + 2) * 2 * c_mid, width), BF),

time: 16.9 us -> 16.3 us (0.964)
  Pallas kernels: 14.8 us -> 14.2 us
    pallas_call x1, Pallas kernels: 14.8 us -> 14.2 us  [one_layer_of_tiles(): pl.pallas_call(functools.partial(tile_kernel, sizes), out_shape=jax.Shape...]
where the time goes in v4:
time: 16.3 us; the launch traced here: 16.1 us
  Pallas kernels  14.2 us (87%)
  local copies, waits for them, and re-layouts  1.88 us (12%)
    pallas_call x1, Pallas kernels, one_layer_of_tiles(): pl.pallas_call(functools.partial(tile_kernel, sizes), out_shape=jax.Shape...  14.2 us
    unnamed x1, local copies, waits for them, and re-layouts  1.88 us

profile of v4, /device:TPU:0, one launch (start us, length us, event | category | flops | bytes accessed | tf_op | source)
XLA Modules:
  0.0 16.1 jit_solution(13974548397583350408)
XLA Ops:
  0.0 14.2 %shard_map.37 = bf16[16,2,16,512]{3,2,1,0:T(8,128)(2,1)} custom-call(bf16[32,2,16,512]{3,2,1,0:T(8,128)(2,1)} %vox_hbm.1, bf16[3,3,3,16,32]{4,3,2,1,0:T(8,128)(2,1)} %first_hbm.1, bf16[3,3,3,16,64]{4,3,2,1,0:T(8,128)(2,1)} %second_hbm.1), custom_call_target="tpu_custom_call" | custom-call | tf_op jit(solution)/shard_map/pallas_call | solution.py:297
  14.2 1.9 %copy.5 = bf16[16,2,16,512]{3,2,1,0:T(8,128)(2,1)} copy(bf16[16,2,16,512]{3,2,1,0:T(8,128)(2,1)} %shard_map.37) | data formatting | bytes 1048576

commit v5 on v4

--- a/solution.py
+++ b/solution.py
@@ -256,19 +256,6 @@
     for k in range(1, n_chan):
         lay_filters(k)
     lax.fori_loop(2, height - 1, lambda r, _: layer_one(r, 1, n_chan), None, unroll=13)
-    for copy in halos:
-        copy.wait()
-
-    for edge, start in ((0, 0), (n_space - 1, height + 2)):
-        at = pl.ds(start * c_in, 2 * c_in)
-        xs[:, at, :] = jnp.where(position == edge, jnp.zeros((), BF), xs[:, at, :])
-    lax.fori_loop(0, 2, lambda r, _: layer_one(r, 0, n_chan), None, unroll=3)
-    lax.fori_loop(height - 1, height + 2, lambda r, _: layer_one(r, 0, n_chan), None, unroll=3)
-
-    for edge, start in ((0, 0), (n_space - 1, height + 1)):
-        at = pl.ds(start * 2 * c_mid, 2 * c_mid)
-        hid[at, :] = jnp.where(position == edge, jnp.zeros((), BF), hid[at, :])
-
     def layer_two(r):
         window = pl.ds(pl.multiple_of(r * 2 * c_mid, 2 * c_mid), 6 * c_mid)
         product = jnp.dot(w2[...], hid[window, :], preferred_element_type=F32)
@@ -279,7 +266,22 @@
                     d * own : (d + 1) * own, t * LANES : (t + 1) * LANES
                 ]
 
-    lax.fori_loop(0, height, lambda r, _: layer_two(r), None, unroll=16)
+    lax.fori_loop(2, height - 3, lambda r, _: layer_two(r), None, unroll=11)
+    for copy in halos:
+        copy.wait()
+
+    for edge, start in ((0, 0), (n_space - 1, height + 2)):
+        at = pl.ds(start * c_in, 2 * c_in)
+        xs[:, at, :] = jnp.where(position == edge, jnp.zeros((), BF), xs[:, at, :])
+    lax.fori_loop(0, 2, lambda r, _: layer_one(r, 0, n_chan), None, unroll=3)
+    lax.fori_loop(height - 1, height + 2, lambda r, _: layer_one(r, 0, n_chan), None, unroll=3)
+
+    for edge, start in ((0, 0), (n_space - 1, height + 1)):
+        at = pl.ds(start * 2 * c_mid, 2 * c_mid)
+        hid[at, :] = jnp.where(position == edge, jnp.zeros((), BF), hid[at, :])
+
+    for r in (0, 1, height - 3, height - 2, height - 1):
+        layer_two(r)
     for d in range(2):
         for o in range(own):
             for t in range(tiles):

time: 16.3 us -> 16.4 us (level)
  no operation moved by 1% of the time
where the time goes in v5:
time: 16.4 us; the launch traced here: 16.2 us
  Pallas kernels  14.3 us (87%)
  local copies, waits for them, and re-layouts  1.88 us (11%)
    pallas_call x1, Pallas kernels, one_layer_of_tiles(): pl.pallas_call(functools.partial(tile_kernel, sizes), out_shape=jax.Shape...  14.3 us
    unnamed x1, local copies, waits for them, and re-layouts  1.88 us

profile of v5, /device:TPU:0, one launch (start us, length us, event | category | flops | bytes accessed | tf_op | source)
XLA Modules:
  0.0 16.2 jit_solution(12570565426105176731)
XLA Ops:
  0.0 14.3 %shard_map.37 = bf16[16,2,16,512]{3,2,1,0:T(8,128)(2,1)} custom-call(bf16[32,2,16,512]{3,2,1,0:T(8,128)(2,1)} %vox_hbm.1, bf16[3,3,3,16,32]{4,3,2,1,0:T(8,128)(2,1)} %first_hbm.1, bf16[3,3,3,16,64]{4,3,2,1,0:T(8,128)(2,1)} %second_hbm.1), custom_call_target="tpu_custom_call" | custom-call | tf_op jit(solution)/shard_map/pallas_call | solution.py:299
  14.3 1.9 %copy.5 = bf16[16,2,16,512]{3,2,1,0:T(8,128)(2,1)} copy(bf16[16,2,16,512]{3,2,1,0:T(8,128)(2,1)} %shard_map.37) | data formatting | bytes 1048576
